TPU v7x, 256 devices: a whole 4x4x8 slice. The times are simulated.
256 devices in a mesh: leaf: 16 (over z, core), row: 4 (over y), col: 4 (over x).
Axes of the slice: x: 4, y: 4, z: 8, core: 2. Of those that a mesh axis runs over, the one named last changes fastest.
Arguments:
- sketch_leaf: bfloat16 [131072, 256], P(('leaf', 'row'), 'col'), may hold values from -6 to 6
- sketch_sep: bfloat16 [8192, 256], P(('row', 'col')), may hold values from -6 to 6
- leaf_inverse: bfloat16 [131072, 8192], P(('leaf', 'col'), 'row'), as said below
- coupling: bfloat16 [131072, 2048], P(('leaf', 'col'), 'row'), may hold values from -0.0625 to 0.0625
- sep_inverse: bfloat16 [8192, 8192], P('leaf', ('row', 'col'))
- front_map: int32 [16, 16], replicated, may hold values from 0 to 63, as said below
Outputs:
- sketch_out_leaf: float32 [131072, 256], P(('leaf', 'row'), 'col')
- sketch_out_sep: float32 [8192, 256], P(('row', 'col'))
Inputs may be any that keep to these rules, and one draw needn't show every extreme that they name: `front_map`: row block q of every section's coupling lies in separator blocks q * 4 to q * 4 + 3. leaf_inverse and sep_inverse are inverses of lower triangular factor blocks (in natural order), stored in block-cyclic order.
All inputs are finite; a program needn't handle non-finite values.
Results may differ from a plain program's by a relative error of at most 0.024.
Values may be sent and summed in bfloat16 or wider, within the bound.
A program may use at most 64 MiB of HBM per device.

v0:
```python
import jax
import jax.numpy as jnp
from jax import lax
from jax.sharding import PartitionSpec as P


def contract_rows(left, right):
    return lax.dot_general(
        left, right, (((0,), (0,)), ((), ())), preferred_element_type=jnp.float32
    )


def shards(sketch_leaf, sketch_sep, leaf_inverse, coupling, sep_inverse, front_map):
    columns = sketch_leaf.shape[1] * lax.axis_size("col")
    q_index = lax.axis_index("row") * lax.axis_size("col") + lax.axis_index("col")
    section = lax.axis_index("leaf")
    partial_value = jnp.dot(
        leaf_inverse,
        lax.all_gather(sketch_leaf, "col", axis=1, tiled=True),
        preferred_element_type=jnp.float32,
    )
    front_z = lax.psum_scatter(partial_value, "row", scatter_dimension=1, tiled=True).astype(
        jnp.bfloat16
    )
    coupled_part = contract_rows(coupling, lax.all_gather(front_z, "row", axis=1, tiled=True))
    coupled = lax.psum_scatter(coupled_part, "col", scatter_dimension=0, tiled=True).astype(
        jnp.bfloat16
    )
    block_rows = coupled.shape[0]
    group = sketch_sep.shape[0] // block_rows
    own_slot = front_map[section, q_index] - q_index * group
    place = (jnp.arange(group, dtype=jnp.int32) == own_slot).astype(jnp.float32)
    spread = (place[:, None, None] * coupled.astype(jnp.float32)[None]).reshape(
        group * block_rows, columns
    )
    total = lax.psum(spread.astype(jnp.bfloat16), "leaf").astype(jnp.float32)
    sep_rhs = (sketch_sep.astype(jnp.float32) - total).astype(jnp.bfloat16)
    sep_part = jnp.dot(sep_inverse, sep_rhs, preferred_element_type=jnp.float32)
    sep_mid = lax.psum(sep_part.astype(jnp.bfloat16), ("row", "col"))
    sketch_out_sep = lax.psum(
        contract_rows(sep_inverse, sep_mid).astype(jnp.bfloat16), "leaf"
    ).astype(jnp.float32)
    sep_round = sketch_out_sep.astype(jnp.bfloat16)
    pulled = lax.dynamic_slice_in_dim(sep_round, own_slot * block_rows, block_rows, 0)
    back_part = jnp.dot(
        coupling,
        lax.all_gather(pulled, "col", axis=0, tiled=True),
        preferred_element_type=jnp.float32,
    )
    back_slice = lax.psum_scatter(
        back_part.astype(jnp.bfloat16), "row", scatter_dimension=1, tiled=True
    ).astype(jnp.float32)
    leaf_rhs = (front_z.astype(jnp.float32) - back_slice).astype(jnp.bfloat16)
    out_part = contract_rows(leaf_inverse, lax.all_gather(leaf_rhs, "row", axis=1, tiled=True))
    sketch_out_leaf = lax.psum_scatter(
        out_part.astype(jnp.bfloat16), "col", scatter_dimension=1, tiled=True
    ).astype(jnp.float32)
    return (sketch_out_leaf, sketch_out_sep)


def solution(mesh):
    placed = (
        P(("leaf", "row"), "col"),
        P(("row", "col"), None),
        P(("leaf", "col"), "row"),
        P(("leaf", "col"), "row"),
        P("leaf", ("row", "col")),
        P(),
    )
    return jax.shard_map(
        shards,
        mesh=mesh,
        in_specs=placed,
        out_specs=(P(("leaf", "row"), "col"), P(("row", "col"), None)),
        check_vma=False,
    )
```

profile of v0, /device:TPU:8, one launch (start us, length us, event | category | flops | bytes accessed | tf_op | source)
XLA Modules:
  0.0 567.1 jit_solution(8834700790642962263)
XLA Ops:
  7.2 0.0 copy-start
  7.2 0.0 all-gather.4.cloned.1.call-start
  7.2 0.7 all-gather.4.cloned.1.call-update
  7.9 0.0 reduce-scatter.5.cloned.1.call-start
  8.0 31.3 %all-gather.4.cloned.1.call-done = bf16[2048,256]{0,1:T(8,128)(2,1)} async-done(((bf16[2048,64]{0,1:T(8,128)(2,1)}), bf16[2048,256]{0,1:T(8,128)(2,1)}) %all-gather.4.cloned.1.call-update) | async-done | bytes 1048592 | tf_op jit(solution)/shard_map/all_gather | solution.py:19
  39.2 7.3 %fusion.5 = f32[2048,256]{0,1:T(8,128)} fusion(bf16[2048,2048]{1,0:T(8,128)(2,1)} %param.8, bf16[2048,256]{0,1:T(8,128)(2,1)} %all-gather.4.cloned.1.call-done), kind=kOutput, calls=%fused_computation.17 | convolution fusion | flops 2147483648 | bytes 11534336 | tf_op jit(solution)/shard_map/dot_general | solution.py:17
  46.5 0.0 reduce-scatter.5.cloned.1.call-update
  46.6 0.0 all-gather.6.cloned.1.call-start
  46.6 31.5 %reduce-scatter.5.cloned.1.call-done = f32[2048,64]{0,1:T(8,128)} async-done(((f32[2048,256]{0,1:T(8,128)}), f32[2048,64]{0,1:T(8,128)}) %reduce-scatter.5.cloned.1.call-update) | async-done | bytes 524304 | tf_op jit(solution)/shard_map/reduce_scatter | solution.py:22
  78.1 1.8 convert_element_type.68
  79.9 0.0 all-gather.6.cloned.1.call-update
  79.9 0.0 reduce-scatter.7.cloned.1.call-start
  80.0 27.3 %all-gather.6.cloned.1.call-done = bf16[2048,256]{0,1:T(8,128)(2,1)} async-done(((bf16[2048,64]{0,1:T(8,128)(2,1)}), bf16[2048,256]{0,1:T(8,128)(2,1)}) %all-gather.6.cloned.1.call-update) | async-done | bytes 1048592 | tf_op jit(solution)/shard_map/all_gather | solution.py:25
  107.3 2.7 convolution_bitcast_fusion
  110.0 0.0 reduce-scatter.7.cloned.1.call-update
  110.0 0.0 all-reduce.4.cloned.1.call-start
  110.1 1.3 dynamic_slice.6
  112.0 0.1 broadcast_bitcast_fusion
  112.1 23.5 %reduce-scatter.7.cloned.1.call-done = f32[128,256]{0,1:T(8,128)} async-done(((f32[512,256]{0,1:T(8,128)}), f32[128,256]{0,1:T(8,128)}) %reduce-scatter.7.cloned.1.call-update) | async-done | bytes 131088 | tf_op jit(solution)/shard_map/reduce_scatter | solution.py:26
  135.6 0.9 convert_convert_fusion
  136.5 0.1 copy.8
  136.6 0.8 fusion.4
  137.4 0.0 all-reduce.4.cloned.1.call-update
  137.5 0.0 all-reduce.6.cloned.1.call-start
  137.5 109.2 %all-reduce.4.cloned.1.call-done = bf16[512,256]{1,0:T(8,128)(2,1)} async-done(((bf16[512,256]{1,0:T(8,128)(2,1)}), bf16[512,256]{1,0:T(8,128)(2,1)}) %all-reduce.4.cloned.1.call-update) | async-done | bytes 262160 | tf_op jit(solution)/shard_map/psum | solution.py:36
  246.7 2.0 fusion.2
  248.7 0.0 all-reduce.6.cloned.1.call-update
  248.7 0.0 all-reduce.8.cloned.1.call-start
  248.8 95.9 %all-reduce.6.cloned.1.call-done = bf16[512,256]{0,1:T(8,128)(2,1)} async-done(((bf16[512,256]{0,1:T(8,128)(2,1)}), bf16[512,256]{0,1:T(8,128)(2,1)}) %all-reduce.6.cloned.1.call-update) | async-done | bytes 262160 | tf_op jit(solution)/shard_map/psum | solution.py:39
  344.7 2.0 fusion.3
  346.6 0.0 all-reduce.8.cloned.1.call-update
  346.7 0.0 reduce-scatter.9.cloned.1.call-start
  346.7 109.1 %all-reduce.8.cloned.1.call-done = bf16[512,256]{0,1:T(8,128)(2,1)} async-done(((bf16[512,256]{0,1:T(8,128)(2,1)}), bf16[512,256]{0,1:T(8,128)(2,1)}) %all-reduce.8.cloned.1.call-update) | async-done | bytes 262160 | tf_op jit(solution)/shard_map/psum | solution.py:40
  455.8 0.8 constant_dynamic-slice_fusion
  456.7 12.0 %all_gather.14 = bf16[512,256]{0,1:T(8,128)(2,1)S(1)} all-gather(bf16[128,256]{0,1:T(8,128)(2,1)S(1)} %constant_dynamic-slice_fusion), channel_id=1, replica_groups=mesh['leaf'=16,'row'=4,'col'=4] {'col'}, dimensions={0}, use_global_device_ids=true | all-gather | bytes 327680 | tf_op jit(solution)/shard_map/all_gather | solution.py:47
  468.7 1.7 fusion.1
  470.4 0.0 reduce-scatter.9.cloned.1.call-update
  470.4 0.0 all-gather.8.cloned.1.call-start
  470.5 23.6 %reduce-scatter.9.cloned.1.call-done = bf16[2048,64]{0,1:T(8,128)(2,1)} async-done(((bf16[2048,256]{0,1:T(8,128)(2,1)}), bf16[2048,64]{0,1:T(8,128)(2,1)}) %reduce-scatter.9.cloned.1.call-update) | async-done | bytes 262160 | tf_op jit(solution)/shard_map/reduce_scatter | solution.py:50
  494.0 1.7 subtract_convert_fusion
  495.7 0.0 all-gather.8.cloned.1.call-update
  495.7 0.0 reduce-scatter.11.cloned.1.call-start
  495.8 28.2 %all-gather.8.cloned.1.call-done = bf16[2048,256]{0,1:T(8,128)(2,1)} async-done(((bf16[2048,64]{0,1:T(8,128)(2,1)}), bf16[2048,256]{0,1:T(8,128)(2,1)}) %all-gather.8.cloned.1.call-update) | async-done | bytes 1048592 | tf_op jit(solution)/shard_map/all_gather | solution.py:54
  524.0 7.0 %fusion = bf16[2048,256]{0,1:T(8,128)(2,1)} fusion(bf16[2048,256]{0,1:T(8,128)(2,1)} %all-gather.8.cloned.1.call-done, bf16[2048,2048]{1,0:T(8,128)(2,1)} %param.8), kind=kOutput, calls=%fused_computation.2 | convolution fusion | flops 2148007936 | bytes 10485760 | tf_op jit(solution)/shard_map/dot_general | solution.py:8
  531.0 0.0 reduce-scatter.11.cloned.1.call-update
  531.0 0.9 copy.9
  532.0 26.5 %reduce-scatter.11.cloned.1.call-done = bf16[2048,64]{0,1:T(8,128)(2,1)} async-done(((bf16[2048,256]{0,1:T(8,128)(2,1)}), bf16[2048,64]{0,1:T(8,128)(2,1)}) %reduce-scatter.11.cloned.1.call-update) | async-done | bytes 262160 | tf_op jit(solution)/shard_map/reduce_scatter | solution.py:55
  558.5 1.8 convert_element_type.87
  (10 shorter events, 0.0 us)
Async XLA Ops:
  7.2 100.1 %copy-start = (bf16[2048,512]{1,0:T(8,128)(2,1)S(1)}, bf16[2048,512]{1,0:T(8,128)(2,1)}, u32[]{:S(2)}) copy-start(bf16[2048,512]{1,0:T(8,128)(2,1)} %param.9) | copy-start | bytes 6291460
  7.2 32.1 %all-gather.4.cloned.1.call-start = ((), (), s32[]{:S(2)}) async-start(), calls=%async_computation.4 | async-start | bytes 1310720 | tf_op jit(solution)/shard_map/all_gather | solution.py:19
  7.9 70.2 %reduce-scatter.5.cloned.1.call-start = ((), (), s32[]{:S(2)}) async-start(), calls=%async_computation.5 | async-start | bytes 2621440 | tf_op jit(solution)/shard_map/reduce_scatter | solution.py:22
  46.6 60.7 %all-gather.6.cloned.1.call-start = ((), (), s32[]{:S(2)}) async-start(), calls=%async_computation.6 | async-start | bytes 1310720 | tf_op jit(solution)/shard_map/all_gather | solution.py:25
  79.9 166.8 %copy-start.1 = (bf16[512,512]{1,0:T(8,128)(2,1)S(1)}, bf16[512,512]{1,0:T(8,128)(2,1)}, u32[]{:S(2)}) copy-start(bf16[512,512]{1,0:T(8,128)(2,1)} %param.10) | copy-start | bytes 1572868
  79.9 166.8 %copy-start.4 = (bf16[512,256]{1,0:T(8,128)(2,1)S(1)}, bf16[512,256]{1,0:T(8,128)(2,1)}, u32[]{:S(2)}) copy-start(bf16[512,256]{1,0:T(8,128)(2,1)} %param.7) | copy-start | bytes 786436
  79.9 55.7 %reduce-scatter.7.cloned.1.call-start = ((), (), s32[]{:S(2)}) async-start(), calls=%async_computation.7 | async-start | bytes 655360 | tf_op jit(solution)/shard_map/reduce_scatter | solution.py:26
  110.0 136.7 %all-reduce.4.cloned.1.call-start = ((), (), s32[]{:S(2)}) async-start(), calls=%async_computation.8 | async-start | bytes 524288 | tf_op jit(solution)/shard_map/psum | solution.py:36
  137.5 207.2 %all-reduce.6.cloned.1.call-start = ((), (), s32[]{:S(2)}) async-start(), calls=%async_computation.9 | async-start | bytes 524288 | tf_op jit(solution)/shard_map/psum | solution.py:39
  248.7 207.1 %all-reduce.8.cloned.1.call-start = ((), (), s32[]{:S(2)}) async-start(), calls=%async_computation.10 | async-start | bytes 524288 | tf_op jit(solution)/shard_map/psum | solution.py:40
  346.7 147.3 %reduce-scatter.9.cloned.1.call-start = ((), (), s32[]{:S(2)}) async-start(), calls=%async_computation.11 | async-start | bytes 1310720 | tf_op jit(solution)/shard_map/reduce_scatter | solution.py:50
  468.7 25.4 %copy-start.2 = (f32[2048,64]{0,1:T(8,128)S(1)}, f32[2048,64]{0,1:T(8,128)}, u32[]{:S(2)}) copy-start(f32[2048,64]{0,1:T(8,128)} %reduce-scatter.5.cloned.1.call-done) | copy-start | bytes 1572868
  470.4 53.6 %all-gather.8.cloned.1.call-start = ((), (), s32[]{:S(2)}) async-start(), calls=%async_computation.12 | async-start | bytes 1310720 | tf_op jit(solution)/shard_map/all_gather | solution.py:54
  495.7 35.3 %copy-start.3 = (bf16[512,256]{0,1:T(8,128)(2,1)S(1)}, bf16[512,256]{0,1:T(8,128)(2,1)}, u32[]{:S(2)}) copy-start(bf16[512,256]{0,1:T(8,128)(2,1)} %all-reduce.8.cloned.1.call-done) | copy-start | bytes 786436
  495.7 62.8 %reduce-scatter.11.cloned.1.call-start = ((), (), s32[]{:S(2)}) async-start(), calls=%async_computation.13 | async-start | bytes 1310720 | tf_op jit(solution)/shard_map/reduce_scatter | solution.py:55
Sparse Core Ops, SparseCore 0:
  9.8 29.3 all-gather.3
  46.7 31.3 reduce-scatter.4
  80.6 26.5 all-gather.5
  110.4 25.1 reduce-scatter.6
  138.4 108.2 all-reduce.3
  250.3 94.3 all-reduce.5
  347.7 108.0 all-reduce.7
  470.5 23.4 reduce-scatter.8
  496.5 27.3 all-gather.7
  531.1 27.3 reduce-scatter.10
where the time goes:
time: 568 us; the launch traced here: 567 us
  waiting for transfers between devices  507 us (89%)
  matrix products  22.8 us (4%)
  between operations  14.9 us (3%)
  blocking collectives  12 us (2%)
  other arithmetic  7 us (1%)
    psum x1, waiting for transfers between devices, shards(): total = lax.psum(spread.astype(jnp.bfloat16), 'leaf').astype(jnp.float32)  109 us
    psum x1, waiting for transfers between devices, shards(): lax.psum(contract_rows(sep_inverse, sep_mid).astype(jnp.bfloat16), 'leaf')  109 us
    psum x1, waiting for transfers between devices, shards(): sep_mid = lax.psum(sep_part.astype(jnp.bfloat16), ('row', 'col'))  95.9 us
    reduce_scatter x1, waiting for transfers between devices, shards(): lax.psum_scatter(partial_value, 'row', scatter_dimension=1, tiled=True)  31.5 us
    all_gather x1, waiting for transfers between devices, shards(): lax.all_gather(sketch_leaf, 'col', axis=1, tiled=True)  31.3 us
    all_gather x1, waiting for transfers between devices, shards(): lax.all_gather(leaf_rhs, 'row', axis=1, tiled=True)  28.2 us
    all_gather x1, waiting for transfers between devices, shards(): lax.all_gather(front_z, 'row', axis=1, tiled=True)  27.3 us
    reduce_scatter x1, waiting for transfers between devices, shards(): lax.psum_scatter(out_part.astype(jnp.bfloat16), 'col', scatter_dimension=...  26.5 us
  transfers between devices with their start and end apart: 10, of which 10 were waited for; matrix products, arithmetic and copies ran while one was open for 0% of the time, Pallas kernels for 0%

commit v1 on v0

--- a/solution.py
+++ b/solution.py
@@ -36,7 +36,7 @@
     total = lax.psum(spread.astype(jnp.bfloat16), "leaf").astype(jnp.float32)
     sep_rhs = (sketch_sep.astype(jnp.float32) - total).astype(jnp.bfloat16)
     sep_part = jnp.dot(sep_inverse, sep_rhs, preferred_element_type=jnp.float32)
-    sep_mid = lax.psum(sep_part.astype(jnp.bfloat16), ("row", "col"))
+    sep_mid = jnp.sum(lax.all_gather(sep_part.astype(jnp.bfloat16), ("row", "col")), axis=0)
     sketch_out_sep = lax.psum(
         contract_rows(sep_inverse, sep_mid).astype(jnp.bfloat16), "leaf"
     ).astype(jnp.float32)

time: 568 us -> 540 us (0.951)
  waiting for transfers between devices: 507 us -> 473 us
    psum x1 -> x0, waiting for transfers between devices: 95.9 us -> none  [shards(): sep_mid = lax.psum(sep_part.astype(jnp.bfloat16), ('row', 'col'))]
    all_gather x0 -> x1, waiting for transfers between devices: none -> 63.4 us  [shards(): lax.all_gather(sep_part.astype(jnp.bfloat16), ('row', 'col'))]
where the time goes in v1:
time: 540 us; the launch traced here: 539 us
  waiting for transfers between devices  473 us (88%)
  matrix products  21.8 us (4%)
  between operations  14.9 us (3%)
  blocking collectives  12 us (2%)
  other arithmetic  9.54 us (2%)
  local copies, waits for them, and re-layouts  7.29 us (1%)
    psum x1, waiting for transfers between devices, shards(): total = lax.psum(spread.astype(jnp.bfloat16), 'leaf').astype(jnp.float32)  109 us
    psum x1, waiting for transfers between devices, shards(): lax.psum(contract_rows(sep_inverse, sep_mid).astype(jnp.bfloat16), 'leaf')  108 us
    all_gather x1, waiting for transfers between devices, shards(): lax.all_gather(sep_part.astype(jnp.bfloat16), ('row', 'col'))  63.4 us
    reduce_scatter x1, waiting for transfers between devices, shards(): lax.psum_scatter(partial_value, 'row', scatter_dimension=1, tiled=True)  31.5 us
    all_gather x1, waiting for transfers between devices, shards(): lax.all_gather(sketch_leaf, 'col', axis=1, tiled=True)  31.3 us
    all_gather x1, waiting for transfers between devices, shards(): lax.all_gather(leaf_rhs, 'row', axis=1, tiled=True)  27.9 us
    all_gather x1, waiting for transfers between devices, shards(): lax.all_gather(front_z, 'row', axis=1, tiled=True)  27.3 us
    reduce_scatter x1, waiting for transfers between devices, shards(): lax.psum_scatter(out_part.astype(jnp.bfloat16), 'col', scatter_dimension=...  26.5 us
  transfers between devices with their start and end apart: 10, of which 10 were waited for; matrix products, arithmetic and copies ran while one was open for 0% of the time, Pallas kernels for 0%

profile of v1, /device:TPU:8, one launch (start us, length us, event | category | flops | bytes accessed | tf_op | source)
XLA Modules:
  0.0 539.2 jit_solution(5227489508755918257)
XLA Ops:
  7.2 0.0 all-gather.6.cloned.1.call-start
  7.2 0.7 all-gather.6.cloned.1.call-update
  7.9 0.0 reduce-scatter.5.cloned.1.call-start
  8.0 31.3 %all-gather.6.cloned.1.call-done = bf16[2048,256]{0,1:T(8,128)(2,1)} async-done(((bf16[2048,64]{0,1:T(8,128)(2,1)}), bf16[2048,256]{0,1:T(8,128)(2,1)}) %all-gather.6.cloned.1.call-update) | async-done | bytes 1048592 | tf_op jit(solution)/shard_map/all_gather | solution.py:19
  39.2 7.3 %fusion.5 = f32[2048,256]{0,1:T(8,128)} fusion(bf16[2048,2048]{1,0:T(8,128)(2,1)} %param.8, bf16[2048,256]{0,1:T(8,128)(2,1)} %all-gather.6.cloned.1.call-done), kind=kOutput, calls=%fused_computation.18 | convolution fusion | flops 2147483648 | bytes 11534336 | tf_op jit(solution)/shard_map/dot_general | solution.py:17
  46.5 0.0 reduce-scatter.5.cloned.1.call-update
  46.6 0.0 all-gather.8.cloned.1.call-start
  46.6 31.5 %reduce-scatter.5.cloned.1.call-done = f32[2048,64]{0,1:T(8,128)} async-done(((f32[2048,256]{0,1:T(8,128)}), f32[2048,64]{0,1:T(8,128)}) %reduce-scatter.5.cloned.1.call-update) | async-done | bytes 524304 | tf_op jit(solution)/shard_map/reduce_scatter | solution.py:22
  78.1 1.8 convert_element_type.70
  79.9 0.0 reduce-scatter.7.cloned.1.call-start
  80.0 27.3 %all-gather.8.cloned.1.call-done = bf16[2048,256]{0,1:T(8,128)(2,1)} async-done(((bf16[2048,64]{0,1:T(8,128)(2,1)}), bf16[2048,256]{0,1:T(8,128)(2,1)}) %all-gather.8.cloned.1.call-update) | async-done | bytes 1048592 | tf_op jit(solution)/shard_map/all_gather | solution.py:25
  107.3 2.7 convolution_bitcast_fusion
  110.0 0.0 reduce-scatter.7.cloned.1.call-update
  110.0 0.0 all-reduce.3.cloned.1.call-start
  110.1 1.3 dynamic_slice.6
  112.0 0.1 broadcast_bitcast_fusion
  112.1 23.5 %reduce-scatter.7.cloned.1.call-done = f32[128,256]{0,1:T(8,128)} async-done(((f32[512,256]{0,1:T(8,128)}), f32[128,256]{0,1:T(8,128)}) %reduce-scatter.7.cloned.1.call-update) | async-done | bytes 131088 | tf_op jit(solution)/shard_map/reduce_scatter | solution.py:26
  135.6 0.9 convert_convert_fusion
  136.5 0.1 copy.10
  136.6 0.8 fusion.4
  137.4 0.0 all-reduce.3.cloned.1.call-update
  137.5 0.0 all-gather.12.cloned.1.call-start
  137.5 109.2 %all-reduce.3.cloned.1.call-done = bf16[512,256]{1,0:T(8,128)(2,1)} async-done(((bf16[512,256]{1,0:T(8,128)(2,1)}), bf16[512,256]{1,0:T(8,128)(2,1)}) %all-reduce.3.cloned.1.call-update) | async-done | bytes 262160 | tf_op jit(solution)/shard_map/psum | solution.py:36
  246.7 2.0 fusion.2
  248.7 0.0 all-gather.12.cloned.1.call-update
  248.7 0.0 all-reduce.5.cloned.1.call-start
  248.8 63.4 %all-gather.12.cloned.1.call-done = bf16[8192,256]{0,1:T(8,128)(2,1)} async-done(((bf16[512,256]{0,1:T(8,128)(2,1)}), bf16[8192,256]{0,1:T(8,128)(2,1)}) %all-gather.12.cloned.1.call-update) | async-done | bytes 4194320 | tf_op jit(solution)/shard_map/all_gather | solution.py:39
  312.2 4.0 copy.12
  316.2 2.5 bitcast_reduce_fusion
  318.8 1.0 fusion.3
  319.8 0.0 all-reduce.5.cloned.1.call-update
  319.8 0.0 reduce-scatter.9.cloned.1.call-start
  319.9 108.2 %all-reduce.5.cloned.1.call-done = bf16[512,256]{0,1:T(8,128)(2,1)} async-done(((bf16[512,256]{0,1:T(8,128)(2,1)}), bf16[512,256]{0,1:T(8,128)(2,1)}) %all-reduce.5.cloned.1.call-update) | async-done | bytes 262160 | tf_op jit(solution)/shard_map/psum | solution.py:40
  428.1 0.8 constant_dynamic-slice_fusion
  428.9 12.0 %all_gather.22 = bf16[512,256]{0,1:T(8,128)(2,1)S(1)} all-gather(bf16[128,256]{0,1:T(8,128)(2,1)S(1)} %constant_dynamic-slice_fusion), channel_id=1, replica_groups=mesh['leaf'=16,'row'=4,'col'=4] {'col'}, dimensions={0}, use_global_device_ids=true | all-gather | bytes 327680 | tf_op jit(solution)/shard_map/all_gather | solution.py:47
  440.9 1.7 fusion.1
  442.6 0.0 reduce-scatter.9.cloned.1.call-update
  442.6 0.0 all-gather.10.cloned.1.call-start
  442.7 23.6 %reduce-scatter.9.cloned.1.call-done = bf16[2048,64]{0,1:T(8,128)(2,1)} async-done(((bf16[2048,256]{0,1:T(8,128)(2,1)}), bf16[2048,64]{0,1:T(8,128)(2,1)}) %reduce-scatter.9.cloned.1.call-update) | async-done | bytes 262160 | tf_op jit(solution)/shard_map/reduce_scatter | solution.py:50
  466.3 1.7 subtract_convert_fusion
  468.0 0.0 all-gather.10.cloned.1.call-update
  468.0 0.0 reduce-scatter.11.cloned.1.call-start
  468.1 27.9 %all-gather.10.cloned.1.call-done = bf16[2048,256]{0,1:T(8,128)(2,1)} async-done(((bf16[2048,64]{0,1:T(8,128)(2,1)}), bf16[2048,256]{0,1:T(8,128)(2,1)}) %all-gather.10.cloned.1.call-update) | async-done | bytes 1048592 | tf_op jit(solution)/shard_map/all_gather | solution.py:54
  496.0 7.0 %fusion = bf16[2048,256]{0,1:T(8,128)(2,1)} fusion(bf16[2048,256]{0,1:T(8,128)(2,1)} %all-gather.10.cloned.1.call-done, bf16[2048,2048]{1,0:T(8,128)(2,1)} %param.8), kind=kOutput, calls=%fused_computation.3 | convolution fusion | flops 2148007936 | bytes 10485760 | tf_op jit(solution)/shard_map/dot_general | solution.py:8
  503.1 0.0 reduce-scatter.11.cloned.1.call-update
  503.1 0.9 copy.11
  504.0 26.5 %reduce-scatter.11.cloned.1.call-done = bf16[2048,64]{0,1:T(8,128)(2,1)} async-done(((bf16[2048,256]{0,1:T(8,128)(2,1)}), bf16[2048,64]{0,1:T(8,128)(2,1)}) %reduce-scatter.11.cloned.1.call-update) | async-done | bytes 262160 | tf_op jit(solution)/shard_map/reduce_scatter | solution.py:55
  530.5 1.8 convert_element_type.89
  (12 shorter events, 0.1 us)
Async XLA Ops:
  7.2 100.1 %copy-start = (bf16[2048,512]{1,0:T(8,128)(2,1)S(1)}, bf16[2048,512]{1,0:T(8,128)(2,1)}, u32[]{:S(2)}) copy-start(bf16[2048,512]{1,0:T(8,128)(2,1)} %param.9) | copy-start | bytes 6291460
  7.2 32.1 %all-gather.6.cloned.1.call-start = ((), (), s32[]{:S(2)}) async-start(), calls=%async_computation.4 | async-start | bytes 1310720 | tf_op jit(solution)/shard_map/all_gather | solution.py:19
  7.9 70.2 %reduce-scatter.5.cloned.1.call-start = ((), (), s32[]{:S(2)}) async-start(), calls=%async_computation.5 | async-start | bytes 2621440 | tf_op jit(solution)/shard_map/reduce_scatter | solution.py:22
  46.6 60.7 %all-gather.8.cloned.1.call-start = ((), (), s32[]{:S(2)}) async-start(), calls=%async_computation.6 | async-start | bytes 1310720 | tf_op jit(solution)/shard_map/all_gather | solution.py:25
  79.9 166.8 %copy-start.1 = (bf16[512,512]{1,0:T(8,128)(2,1)S(1)}, bf16[512,512]{1,0:T(8,128)(2,1)}, u32[]{:S(2)}) copy-start(bf16[512,512]{1,0:T(8,128)(2,1)} %param.10) | copy-start | bytes 1572868
  79.9 166.8 %copy-start.4 = (bf16[512,256]{1,0:T(8,128)(2,1)S(1)}, bf16[512,256]{1,0:T(8,128)(2,1)}, u32[]{:S(2)}) copy-start(bf16[512,256]{1,0:T(8,128)(2,1)} %param.7) | copy-start | bytes 786436
  79.9 55.7 %reduce-scatter.7.cloned.1.call-start = ((), (), s32[]{:S(2)}) async-start(), calls=%async_computation.7 | async-start | bytes 655360 | tf_op jit(solution)/shard_map/reduce_scatter | solution.py:26
  110.0 136.7 %all-reduce.3.cloned.1.call-start = ((), (), s32[]{:S(2)}) async-start(), calls=%async_computation.8 | async-start | bytes 524288 | tf_op jit(solution)/shard_map/psum | solution.py:36
  137.5 174.7 %all-gather.12.cloned.1.call-start = ((), (), s32[]{:S(2)}) async-start(), calls=%async_computation.13 | async-start | bytes 4456448 | tf_op jit(solution)/shard_map/all_gather | solution.py:39
  248.7 179.3 %all-reduce.5.cloned.1.call-start = ((), (), s32[]{:S(2)}) async-start(), calls=%async_computation.9 | async-start | bytes 524288 | tf_op jit(solution)/shard_map/psum | solution.py:40
  319.8 146.5 %reduce-scatter.9.cloned.1.call-start = ((), (), s32[]{:S(2)}) async-start(), calls=%async_computation.10 | async-start | bytes 1310720 | tf_op jit(solution)/shard_map/reduce_scatter | solution.py:50
  440.9 25.4 %copy-start.2 = (f32[2048,64]{0,1:T(8,128)S(1)}, f32[2048,64]{0,1:T(8,128)}, u32[]{:S(2)}) copy-start(f32[2048,64]{0,1:T(8,128)} %reduce-scatter.5.cloned.1.call-done) | copy-start | bytes 1572868
  442.6 53.4 %all-gather.10.cloned.1.call-start = ((), (), s32[]{:S(2)}) async-start(), calls=%async_computation.11 | async-start | bytes 1310720 | tf_op jit(solution)/shard_map/all_gather | solution.py:54
  468.0 35.1 %copy-start.3 = (bf16[512,256]{0,1:T(8,128)(2,1)S(1)}, bf16[512,256]{0,1:T(8,128)(2,1)}, u32[]{:S(2)}) copy-start(bf16[512,256]{0,1:T(8,128)(2,1)} %all-reduce.5.cloned.1.call-done) | copy-start | bytes 786436
  468.0 62.5 %reduce-scatter.11.cloned.1.call-start = ((), (), s32[]{:S(2)}) async-start(), calls=%async_computation.12 | async-start | bytes 1310720 | tf_op jit(solution)/shard_map/reduce_scatter | solution.py:55
Sparse Core Ops, SparseCore 0:
  9.8 29.3 all-gather.5
  46.7 31.3 reduce-scatter.4
  80.6 26.5 all-gather.7
  110.4 25.1 reduce-scatter.6
  138.4 108.2 all-reduce.2
  249.5 62.5 all-gather.11
  319.9 108.0 all-reduce.4
  442.8 23.4 reduce-scatter.8
  468.7 27.2 all-gather.9
  503.2 27.2 reduce-scatter.10
